TPU v7x, 32 devices: a whole 2x2x4 slice. The times are simulated.
32 devices in a mesh: groups: 2 (over y), dp: 4 (over z), pipe: 2 (over core), tensor: 2 (over x).
Axes of the slice: x: 2, y: 2, z: 4, core: 2. Of those that a mesh axis runs over, the one named last changes fastest.
Arguments:
- layer_inputs: bfloat16 [2, 4096, 5120], P('pipe', ('groups', 'dp'), 'tensor'), parts along dimension 1, may hold values from -6 to 6
- output_grads: bfloat16 [2, 4096, 5120], P('pipe', ('groups', 'dp', 'tensor')), parts along dimension 1, may hold values from -6 to 6
- proj_in: bfloat16 [2, 64, 5120], P('pipe', None, 'tensor'), may hold values from -0.078125 to 0.078125
- proj_out: bfloat16 [2, 64, 5120], P('pipe'), may hold values from -0.078125 to 0.078125
- counts: int32 [8], P(('groups', 'dp')), parts along dimension 0, may hold values from 1 to 512, 1536 in all
- token_mask: int32 [4096], P(('groups', 'dp')), parts along dimension 0, may hold values 0 or 1
- precond_out: float32 [2, 64, 64], P('pipe'), may hold values from -1 to 3
- precond_in: float32 [2, 64, 64], P('pipe'), may hold values from -1 to 3
- queries: bfloat16 [256, 2, 64, 64], P('dp', 'pipe', 'tensor'), may hold values from -0.0029296875 to 0.0029296875
- query_ids: int32 [512], P(('groups', 'dp', 'pipe', 'tensor')), parts along dimension 0, may hold values from -1 to 3, as said below
Outputs:
- scores: float32 [256, 8], P(('dp', 'pipe', 'tensor'), 'groups'), parts along dimension 1
There are 2 independent parts, one for each index of `groups`. A program takes and returns all parts, laid end to end along the dimension named above; an argument that names none is the same for every part. Nothing has to cross between parts.
Inputs may be any that keep to these rules, and one draw needn't show every extreme that they name: `counts`: the 4 entries of one group sum to 1536. `query_ids`: about half of the entries are -1.
All inputs are finite; a program needn't handle non-finite values. No bound on the sum of `token_mask` on one device may be relied on, other than what follows from the above.
Results may differ from a plain program's by a relative error of at most 0.003.
Values may be sent and summed in bfloat16 or wider, within the bound.
A program may use at most 64 MiB of HBM per device.

v0:
```python
import jax
import jax.numpy as jnp
from jax import lax
from jax.sharding import PartitionSpec as P


def local(
    layer_inputs,
    output_grads,
    proj_in,
    proj_out,
    counts,
    token_mask,
    precond_out,
    precond_in,
    queries,
    query_ids,
):
    highest = lax.Precision.HIGHEST
    inputs_local = layer_inputs[0]
    grads_local = output_grads[0]
    tok_rows = inputs_local.shape[0]
    seq_count = counts.shape[0]
    seq_len = tok_rows // seq_count
    rank_full = proj_in.shape[1]
    part_in = jnp.dot(inputs_local, proj_in[0].T, preferred_element_type=jnp.float32)
    own_out = jnp.dot(grads_local, proj_out[0].T, preferred_element_type=jnp.float32)
    full_out = lax.all_gather(own_out, "tensor", axis=0, tiled=True)
    slots = jnp.arange(tok_rows, dtype=jnp.int32)
    position = slots % seq_len
    owner = slots // seq_len
    matches = owner[:, None] == jnp.arange(seq_count, dtype=jnp.int32)[None, :]
    limit = jnp.sum(jnp.where(matches, counts[None, :], 0), axis=1)
    weight = jnp.where((position < limit) & (token_mask == 1), 1.0, 0.0).astype(jnp.float32)
    weighted = (full_out * weight[:, None]).reshape(seq_count, seq_len, rank_full)
    full_in = lax.psum(part_in, "tensor")
    grads = jnp.einsum(
        "esr,esc->erc", weighted, full_in.reshape(seq_count, seq_len, rank_full), precision=highest
    )
    left = jnp.einsum("ab,ebc->eac", precond_out[0], grads, precision=highest)
    precond = jnp.einsum("eac,cd->ead", left, precond_in[0], precision=highest)
    row_count = rank_full // lax.axis_size("tensor")
    row_start = lax.axis_index("tensor") * row_count
    own_rows = lax.dynamic_slice_in_dim(precond, row_start, row_count, 1).astype(jnp.bfloat16)
    train_flat = own_rows.reshape(seq_count, row_count * rank_full)
    query_flat = queries[:, 0].reshape(queries.shape[0], row_count * rank_full)
    partial_scores = jnp.dot(
        lax.all_gather(query_flat, "dp", axis=0, tiled=True),
        train_flat.T,
        preferred_element_type=jnp.float32,
    )
    dp_count = lax.axis_size("dp")
    partial_scores = partial_scores.reshape(dp_count, query_flat.shape[0], seq_count)
    summed = lax.psum_scatter(partial_scores, ("pipe", "tensor"), scatter_dimension=1, tiled=True)
    moved = lax.all_to_all(summed, "dp", split_axis=0, concat_axis=2, tiled=True)
    scores = moved[0]
    hits = query_ids[:, None] == jnp.arange(scores.shape[1], dtype=jnp.int32)[None, :]
    return jnp.where(hits, 0.0, scores)


def solution(mesh):
    placed = (
        P("pipe", ("groups", "dp"), "tensor"),
        P("pipe", ("groups", "dp", "tensor"), None),
        P("pipe", None, "tensor"),
        P("pipe", None, None),
        P(("groups", "dp")),
        P(("groups", "dp")),
        P("pipe", None, None),
        P("pipe", None, None),
        P("dp", "pipe", "tensor", None),
        P(("groups", "dp", "pipe", "tensor")),
    )
    return jax.shard_map(
        local,
        mesh=mesh,
        in_specs=placed,
        out_specs=P(("dp", "pipe", "tensor"), "groups"),
        check_vma=False,
    )
```

profile of v0, /device:TPU:0, one launch (start us, length us, event | category | flops | bytes accessed | tf_op | source)
XLA Modules:
  0.0 84.7 jit_solution(13510632668813499170)
XLA Ops:
  7.4 0.0 copy-start
  7.4 0.0 all-reduce.2.cloned.1.call-start
  7.4 1.7 %copy-done = bf16[1,512,2560]{2,1,0:T(8,128)(2,1)S(1)} copy-done((bf16[1,512,2560]{2,1,0:T(8,128)(2,1)S(1)}, bf16[1,512,2560]{2,1,0:T(8,128)(2,1)}, u32[]{:S(2)}) %copy-start) | copy-done | bytes 2621464
  9.1 2.5 %fusion = f32[512,64]{1,0:T(8,128)} fusion(bf16[1,512,2560]{2,1,0:T(8,128)(2,1)S(1)} %copy-done, bf16[1,64,2560]{2,1,0:T(8,128)(2,1)} %param.12), kind=kOutput, calls=%fused_computation | convolution fusion | flops 167772160 | bytes 3080192 | tf_op jit(solution)/shard_map/dot_general | solution.py:26
  11.6 0.0 all-reduce.2.cloned.1.call-update
  11.6 0.0 copy-start.2
  11.6 0.0 copy-start.3
  11.6 0.0 all-gather.2.cloned.1.call-start
  11.7 2.2 %reshape_squeeze.3 = bf16[64,2048]{1,0:T(8,128)(2,1)} reshape(bf16[64,1,32,64]{3,2,1,0:T(8,128)(2,1)} %param.18) | data formatting | bytes 524288 | tf_op jit(solution)/shard_map/reshape;squeeze | solution.py:46
  13.9 0.0 all-gather.2.cloned.1.call-update
  13.9 0.0 reduce-scatter.4.cloned.1.call-start
  14.6 0.0 copy-done.1
  14.6 0.0 copy-start.5
  14.6 2.6 %fusion.2 = f32[256,64]{1,0:T(8,128)S(1)} fusion(bf16[1,256,5120]{2,1,0:T(8,128)(2,1)} %param.11, bf16[1,64,5120]{2,1,0:T(8,128)(2,1)S(1)} %copy-done.1), kind=kOutput, calls=%fused_computation.2 | convolution fusion | flops 167772160 | bytes 3342336 | tf_op jit(solution)/shard_map/dot_general | solution.py:27
  17.2 9.9 %all_gather.6 = f32[512,64]{1,0:T(8,128)S(1)} all-gather(f32[256,64]{1,0:T(8,128)S(1)} %fusion.2), channel_id=1, replica_groups=mesh['groups'=2,'dp'=4,'pipe'=2,'tensor'=2] {'tensor'}, dimensions={0}, use_global_device_ids=true | all-gather | bytes 196608 | tf_op jit(solution)/shard_map/all_gather | solution.py:28
  27.1 0.0 copy-done.4
  27.1 13.1 %all-reduce.2.cloned.1.call-done = f32[512,64]{1,0:T(8,128)} async-done(((f32[512,64]{1,0:T(8,128)}), f32[512,64]{1,0:T(8,128)}) %all-reduce.2.cloned.1.call-update) | async-done | bytes 131088 | tf_op jit(solution)/shard_map/psum | solution.py:36
  40.2 1.6 %fusion.6 = f32[64,64]{1,0:T(8,128)S(1)} fusion(f32[512,64]{1,0:T(8,128)} %all-reduce.2.cloned.1.call-done, f32[512,64]{1,0:T(8,128)S(1)} %all_gather.6, f32[512]{0:T(512)S(1)} %fusion.20), kind=kOutput, calls=%fused_computation.7 | convolution fusion | flops 25198592 | bytes 280576 | tf_op jit(solution)/shard_map/esr,esc->erc/dot_general | solution.py:37
  41.8 0.0 copy-done.2
  41.8 0.2 convolution_bitcast_fusion
  42.1 0.0 copy-done.3
  42.1 0.2 fusion.9
  42.3 0.1 reshape.42
  42.4 2.2 %all-gather.2.cloned.1.call-done = bf16[256,2048]{1,0:T(8,128)(2,1)} async-done(((bf16[64,2048]{1,0:T(8,128)(2,1)}), bf16[256,2048]{1,0:T(8,128)(2,1)}) %all-gather.2.cloned.1.call-update) | async-done | bytes 1048592 | tf_op jit(solution)/shard_map/all_gather | solution.py:48
  44.6 1.7 %fusion.22 = f32[1,4,64]{2,0,1:T(1,128)S(1)} fusion(bf16[2048,1,1]{0,1,2:T(2,128)(2,1)S(1)} %reshape.42, bf16[4,64,2048]{2,1,0:T(8,128)(2,1)} %bitcast.50), kind=kOutput, calls=%fused_computation.30 | convolution fusion | flops 1048576 | bytes 1053696 | tf_op jit(solution)/shard_map/dot_general | solution.py:47
  46.3 0.7 copy.13
  47.0 0.0 reduce-scatter.4.cloned.1.call-update
  47.1 18.9 %reduce-scatter.4.cloned.1.call-done = f32[16,4]{1,0:T(8,128)} async-done(((f32[64,4]{1,0:T(8,128)}), f32[16,4]{1,0:T(8,128)}) %reduce-scatter.4.cloned.1.call-update) | async-done | bytes 272
  66.0 0.8 copy.14
  66.7 9.9 %all_to_all.15 = f32[4,16,1]{1,2,0:T(1,128)S(1)} all-to-all(f32[4,16,1]{1,2,0:T(1,128)S(1)} %bitcast.54), channel_id=1, replica_groups=mesh['groups'=2,'dp'=4,'pipe'=2,'tensor'=2] {'dp'}, dimensions={0} | all-to-all | bytes 512 | tf_op jit(solution)/shard_map/all_to_all | solution.py:55
  76.7 0.0 copy-done.5
  76.7 0.6 fusion.21
  (4 shorter events, 0.0 us)
Async XLA Ops:
  7.4 1.7 %copy-start = (bf16[1,512,2560]{2,1,0:T(8,128)(2,1)S(1)}, bf16[1,512,2560]{2,1,0:T(8,128)(2,1)}, u32[]{:S(2)}) copy-start(bf16[1,512,2560]{2,1,0:T(8,128)(2,1)} %param.10) | copy-start | bytes 7864324
  7.4 7.2 %copy-start.1 = (bf16[1,64,5120]{2,1,0:T(8,128)(2,1)S(1)}, bf16[1,64,5120]{2,1,0:T(8,128)(2,1)}, u32[]{:S(2)}) copy-start(bf16[1,64,5120]{2,1,0:T(8,128)(2,1)} %param.13) | copy-start | bytes 1966084
  7.4 32.8 %all-reduce.2.cloned.1.call-start = ((), (), s32[]{:S(2)}) async-start(), calls=%async_computation.2 | async-start | bytes 524288 | tf_op jit(solution)/shard_map/psum | solution.py:36
  11.6 15.5 %copy-start.4 = (s32[512]{0:T(512)S(1)}, s32[512]{0:T(512)}, u32[]{:S(2)}) copy-start(s32[512]{0:T(512)} %param.15) | copy-start | bytes 6148
  11.6 30.2 %copy-start.2 = (f32[1,64,64]{2,1,0:T(8,128)S(1)}, f32[1,64,64]{2,1,0:T(8,128)}, u32[]{:S(2)}) copy-start(f32[1,64,64]{2,1,0:T(8,128)} %param.16) | copy-start | bytes 49156
  11.6 30.4 %copy-start.3 = (f32[1,64,64]{2,1,0:T(8,128)S(1)}, f32[1,64,64]{2,1,0:T(8,128)}, u32[]{:S(2)}) copy-start(f32[1,64,64]{2,1,0:T(8,128)} %param.17) | copy-start | bytes 49156
  11.6 33.0 %all-gather.2.cloned.1.call-start = ((), (), s32[]{:S(2)}) async-start(), calls=%async_computation.3 | async-start | bytes 1310720 | tf_op jit(solution)/shard_map/all_gather | solution.py:48
  13.9 52.0 %reduce-scatter.4.cloned.1.call-start = ((), (), s32[]{:S(2)}) async-start(), calls=%async_computation.4 | async-start | bytes 40960
  14.6 62.0 %copy-start.5 = (s32[16]{0:T(128)S(1)}, s32[16]{0:T(128)}, u32[]{:S(2)}) copy-start(s32[16]{0:T(128)} %param.19) | copy-start | bytes 196
Sparse Core Ops, SparseCore 0:
  11.7 28.3 all-reduce.1
  47.2 18.7 reduce-scatter.3
Sparse Core Ops, SparseCore 1:
  14.0 30.5 all-gather.1
where the time goes:
time: 85 us; the launch traced here: 84.7 us
  waiting for transfers between devices  34.2 us (40%)
  blocking collectives  19.8 us (23%)
  between operations  15.6 us (18%)
  matrix products  8.87 us (10%)
  local copies, waits for them, and re-layouts  5.55 us (7%)
    unnamed x4, waiting for transfers between devices  18.9 us
    psum x1, waiting for transfers between devices, local(): full_in = lax.psum(part_in, 'tensor')  13.1 us
    all_to_all x1, blocking collectives, local(): lax.all_to_all(summed, 'dp', split_axis=0, concat_axis=2, tiled=True)  9.92 us
    all_gather x1, blocking collectives, local(): full_out = lax.all_gather(own_out, 'tensor', axis=0, tiled=True)  9.9 us
    unnamed x14, local copies, waits for them, and re-layouts  3.26 us
    dot_general x1, matrix products, local(): jnp.dot(grads_local, proj_out[0].T, preferred_element_type=jnp.float32)  2.56 us
    dot_general x1, matrix products, local(): jnp.dot(inputs_local, proj_in[0].T, preferred_element_type=jnp.float32)  2.48 us
    another operation x1, local copies, waits for them, and re-layouts, local(): query_flat = queries[:, 0].reshape(queries.shape[0], row_count * rank_full)  2.19 us
  transfers between devices with their start and end apart: 3, of which 3 were waited for; matrix products, arithmetic and copies ran while one was open for 8% of the time, Pallas kernels for 0%

commit v1 on v0

v1 whole, which is shorter than its diff:
```python
import functools

import jax
import jax.numpy as jnp
from jax import lax
from jax.experimental import pallas as pl
from jax.experimental.pallas import tpu as pltpu
from jax.sharding import PartitionSpec as P

MESH = pl.DeviceIdType.MESH
HIGHEST = lax.Precision.HIGHEST
NT = (((1,), (1,)), ((), ()))


def dot_nt(a, b, precision=None):
    return lax.dot_general(a, b, NT, precision=precision, preferred_element_type=jnp.float32)


def kernel(
    dims,
    x_hbm,
    g_hbm,
    pin_hbm,
    pout_hbm,
    counts_hbm,
    mask_hbm,
    left_hbm,
    right_hbm,
    q_hbm,
    out_ref,
    x_v,
    g_v,
    pin_v,
    pout_v,
    count_s,
    mask_v,
    left_v,
    right_v,
    q_v,
    outs,
    p_send,
    p_recv,
    s_send,
    s_recv,
    load_sem,
    x_sem,
    g_sem,
    a_send_sem,
    a_recv_sem,
    b_send_sem,
    b_recv_sem,
    c_send_sem,
    c_recv_sem,
):
    dp, pipe, tensor, x_chunks, g_chunks = dims
    d, p, t = lax.axis_index("dp"), lax.axis_index("pipe"), lax.axis_index("tensor")
    rank = pout_v.shape[0]
    own_tok = g_v.shape[0]
    rows = rank // tensor
    nq = q_v.shape[0]

    def shift(i, by, size):
        return lax.rem(i + by, size)

    load_pout = pltpu.make_async_copy(pout_hbm.at[0], pout_v, load_sem.at[0])
    load_pout.start()
    g_loads = []
    g_width = g_v.shape[1] // g_chunks
    for c in range(g_chunks):
        cols = pl.ds(c * g_width, g_width)
        load = pltpu.make_async_copy(g_hbm.at[0, :, cols], g_v.at[:, cols], g_sem.at[c])
        load.start()
        g_loads.append(load)
    load_count = pltpu.make_async_copy(counts_hbm, count_s, load_sem.at[1])
    load_mask = pltpu.make_async_copy(mask_hbm, mask_v, load_sem.at[2])
    load_pin = pltpu.make_async_copy(pin_hbm.at[0], pin_v, load_sem.at[3])
    load_count.start()
    load_mask.start()
    load_pin.start()
    x_loads = []
    x_width = x_v.shape[1] // x_chunks
    for c in range(x_chunks):
        cols = pl.ds(c * x_width, x_width)
        load = pltpu.make_async_copy(x_hbm.at[0, :, cols], x_v.at[:, cols], x_sem.at[c])
        load.start()
        x_loads.append(load)
    load_left = pltpu.make_async_copy(left_hbm.at[0], left_v, load_sem.at[4])
    load_right = pltpu.make_async_copy(right_hbm.at[0], right_v, load_sem.at[5])
    load_q = pltpu.make_async_copy(q_hbm.at[:, 0], q_v, load_sem.at[6])
    load_left.start()
    load_right.start()
    load_q.start()

    barrier = pltpu.get_barrier_semaphore()
    block_peers = [(i, j) for i in range(dp) for j in range(tensor) if (i, j) != (0, 0)]
    score_peers = [(i, j) for i in range(pipe) for j in range(tensor) if (i, j) != (0, 0)]
    met = 0
    for i, j in block_peers:
        pl.semaphore_signal(
            barrier, inc=1, device_id={"dp": shift(d, i, dp), "tensor": shift(t, j, tensor)}, device_id_type=MESH
        )
        met += 1
    for i, j in score_peers:
        if i:
            pl.semaphore_signal(
                barrier, inc=1, device_id={"pipe": shift(p, i, pipe), "tensor": shift(t, j, tensor)}, device_id_type=MESH
            )
            met += 1

    load_pout.wait()
    total = jnp.zeros((rank, own_tok), jnp.float32)
    for c in range(g_chunks):
        g_loads[c].wait()
        cols = slice(c * g_width, (c + 1) * g_width)
        total += dot_nt(pout_v[:, cols], g_v[:, cols])
    load_count.wait()
    load_mask.wait()
    start = pl.multiple_of(t * own_tok, own_tok)
    position = start + lax.broadcasted_iota(jnp.int32, (1, own_tok), 1)
    keep = (position < count_s[0]) & (mask_v[:, pl.ds(start, own_tok)] == 1)
    outs[t] = jnp.where(keep, total, 0.0)

    pl.semaphore_wait(barrier, met)
    a_copies = []
    for j in range(1, tensor):
        copy = pltpu.make_async_remote_copy(
            src_ref=outs.at[t],
            dst_ref=outs.at[t],
            send_sem=a_send_sem.at[j],
            recv_sem=a_recv_sem.at[t],
            device_id={"tensor": shift(t, j, tensor)},
            device_id_type=MESH,
        )
        copy.start()
        a_copies.append(copy)

    load_pin.wait()
    ins = jnp.zeros((rank, x_v.shape[0]), jnp.float32)
    for c in range(x_chunks):
        x_loads[c].wait()
        cols = slice(c * x_width, (c + 1) * x_width)
        ins += dot_nt(pin_v[:, cols], x_v[:, cols])
    load_left.wait()
    load_right.wait()
    for j in range(1, tensor):
        source = shift(t, j, tensor)
        pltpu.make_async_remote_copy(
            src_ref=outs.at[source],
            dst_ref=outs.at[source],
            send_sem=a_send_sem.at[j],
            recv_sem=a_recv_sem.at[source],
            device_id={"tensor": source},
            device_id_type=MESH,
        ).wait_recv()
    grads = jnp.zeros((rank, rank), jnp.float32)
    for j in range(tensor):
        grads += dot_nt(outs[j], ins[:, j * own_tok : (j + 1) * own_tok], HIGHEST)
    half = jnp.dot(left_v[...], grads, precision=HIGHEST, preferred_element_type=jnp.float32)
    block = jnp.dot(half, right_v[...], precision=HIGHEST, preferred_element_type=jnp.float32)
    p_send[...] = block.reshape(tensor, rows, rank)

    b_copies = []
    for i, j in block_peers:
        other = shift(t, j, tensor)
        copy = pltpu.make_async_remote_copy(
            src_ref=p_send.at[other],
            dst_ref=p_recv.at[d, t],
            send_sem=b_send_sem.at[i, j],
            recv_sem=b_recv_sem.at[d, t],
            device_id={"dp": shift(d, i, dp), "tensor": other},
            device_id_type=MESH,
        )
        copy.start()
        b_copies.append(copy)
    p_recv[d, t] = p_send[t]
    load_q.wait()
    for i, j in block_peers:
        from_d, from_t = shift(d, i, dp), shift(t, j, tensor)
        pltpu.make_async_remote_copy(
            src_ref=p_send.at[from_t],
            dst_ref=p_recv.at[from_d, from_t],
            send_sem=b_send_sem.at[i, j],
            recv_sem=b_recv_sem.at[from_d, from_t],
            device_id={"dp": from_d, "tensor": from_t},
            device_id_type=MESH,
        ).wait_recv()
    precond = p_recv[:, 0]
    for j in range(1, tensor):
        precond += p_recv[:, j]
    precond = precond.astype(jnp.bfloat16).reshape(dp * rows, rank)

    lanes = dp * rows
    products = dot_nt(q_v[...].reshape(nq * rows, rank), precond).reshape(nq, rows, lanes)
    row = lax.broadcasted_iota(jnp.int32, (rows, lanes), 0)
    lane = lax.broadcasted_iota(jnp.int32, (rows, lanes), 1)
    same = (lax.rem(lane, rows) == row)[None]
    sums = jnp.sum(jnp.where(same, products, 0.0), axis=1)
    s_send[...] = sums.reshape(s_send.shape)

    mine = p * tensor + t
    c_copies = []
    for i, j in score_peers:
        to_p, to_t = shift(p, i, pipe), shift(t, j, tensor)
        copy = pltpu.make_async_remote_copy(
            src_ref=s_send.at[to_p * tensor + to_t],
            dst_ref=s_recv.at[mine],
            send_sem=c_send_sem.at[i, j],
            recv_sem=c_recv_sem.at[mine],
            device_id={"pipe": to_p, "tensor": to_t},
            device_id_type=MESH,
        )
        copy.start()
        c_copies.append(copy)
    s_recv[mine] = s_send[mine]
    for i, j in score_peers:
        from_p, from_t = shift(p, i, pipe), shift(t, j, tensor)
        source = from_p * tensor + from_t
        pltpu.make_async_remote_copy(
            src_ref=s_send.at[source],
            dst_ref=s_recv.at[source],
            send_sem=c_send_sem.at[i, j],
            recv_sem=c_recv_sem.at[source],
            device_id={"pipe": from_p, "tensor": from_t},
            device_id_type=MESH,
        ).wait_recv()
    scores = s_recv[0]
    for i in range(1, pipe * tensor):
        scores += s_recv[i]
    owner = lax.broadcasted_iota(jnp.int32, (dp, lanes), 0)
    lane = lax.broadcasted_iota(jnp.int32, (dp, lanes), 1)
    gather = jnp.where(lax.div(lane, rows) == owner, 1.0, 0.0).astype(jnp.float32)
    out_ref[...] = dot_nt(gather, scores, HIGHEST)
    for copy in a_copies + b_copies + c_copies:
        copy.wait_send()


def cut(width):
    return max(n for n in (1, 2, 3, 4) if width % (n * 128) == 0)


def local(mesh, *args):
    x, g, pin, pout, counts, mask, left, right, queries, query_ids = args
    dp, pipe, tensor = mesh.shape["dp"], mesh.shape["pipe"], mesh.shape["tensor"]
    rank = pin.shape[1]
    rows = rank // tensor
    nq = queries.shape[0]
    parts = pipe * tensor
    lanes = dp * rows
    x_chunks, g_chunks = cut(x.shape[2]), cut(g.shape[2])
    f32, bf16 = jnp.float32, jnp.bfloat16
    hbm = pl.BlockSpec(memory_space=pltpu.HBM)
    dma = pltpu.SemaphoreType.DMA
    scores = pl.pallas_call(
        functools.partial(kernel, (dp, pipe, tensor, x_chunks, g_chunks)),
        out_shape=jax.ShapeDtypeStruct((dp, nq // parts), f32),
        in_specs=[hbm] * 9,
        out_specs=pl.BlockSpec(memory_space=pltpu.VMEM),
        scratch_shapes=[
            pltpu.VMEM(x.shape[1:], bf16),
            pltpu.VMEM(g.shape[1:], bf16),
            pltpu.VMEM(pin.shape[1:], bf16),
            pltpu.VMEM(pout.shape[1:], bf16),
            pltpu.SMEM(counts.shape, jnp.int32),
            pltpu.VMEM((1, mask.shape[0]), jnp.int32),
            pltpu.VMEM((rank, rank), f32),
            pltpu.VMEM((rank, rank), f32),
            pltpu.VMEM((nq, rows, rank), bf16),
            pltpu.VMEM((tensor, rank, g.shape[1]), f32),
            pltpu.VMEM((tensor, rows, rank), f32),
            pltpu.VMEM((dp, tensor, rows, rank), f32),
            pltpu.VMEM((parts, nq // parts, lanes), f32),
            pltpu.VMEM((parts, nq // parts, lanes), f32),
            dma((7,)),
            dma((x_chunks,)),
            dma((g_chunks,)),
            dma((tensor,)),
            dma((tensor,)),
            dma((dp, tensor)),
            dma((dp, tensor)),
            dma((pipe, tensor)),
            dma((parts,)),
        ],
        compiler_params=pltpu.CompilerParams(
            collective_id=0, has_side_effects=True, vmem_limit_bytes=60 * 1024 * 1024
        ),
        name="attribution",
    )(x, g, pin, pout, counts, mask.reshape(1, -1), left, right, queries)
    hits = query_ids[None, :] == jnp.arange(dp, dtype=jnp.int32)[:, None]
    return jnp.where(hits, 0.0, scores).T


def solution(mesh):
    placed = (
        P("pipe", ("groups", "dp"), "tensor"),
        P("pipe", ("groups", "dp", "tensor"), None),
        P("pipe", None, "tensor"),
        P("pipe", None, None),
        P(("groups", "dp")),
        P(("groups", "dp")),
        P("pipe", None, None),
        P("pipe", None, None),
        P("dp", "pipe", "tensor", None),
        P(("groups", "dp", "pipe", "tensor")),
    )
    return jax.shard_map(
        functools.partial(local, mesh),
        mesh=mesh,
        in_specs=placed,
        out_specs=P(("dp", "pipe", "tensor"), "groups"),
        check_vma=False,
    )
```

time: 85 us -> 21.4 us (0.25)
  waiting for transfers between devices: 34.2 us -> 0 us
  blocking collectives: 19.8 us -> 0 us
  Pallas kernels: 0 us -> 19.3 us
  between operations: 15.6 us -> 0.68 us
  matrix products: 8.87 us -> 0 us
  local copies, waits for them, and re-layouts: 5.55 us -> 0.01 us
    pallas_call x0 -> x1, Pallas kernels: none -> 19.3 us  [local(): pl.pallas_call(functools.partial(kernel, (dp, pipe, tensor, x_chunks, g_c...]
    unnamed x4 -> x0, waiting for transfers between devices: 18.9 us -> none
    psum x1 -> x0, waiting for transfers between devices: 13.1 us -> none  [local(): full_in = lax.psum(part_in, 'tensor')]
    all_to_all x1 -> x0, blocking collectives: 9.92 us -> none  [local(): lax.all_to_all(summed, 'dp', split_axis=0, concat_axis=2, tiled=True)]
    all_gather x1 -> x0, blocking collectives: 9.9 us -> none  [local(): full_out = lax.all_gather(own_out, 'tensor', axis=0, tiled=True)]
    dot_general x6 -> x0, matrix products: 8.87 us -> none  [the longest x1 2.56 us: local(): jnp.dot(grads_local, proj_out[0].T, preferred_element_type=jnp.float32)]
    unnamed x14 -> x2, local copies, waits for them, and re-layouts: 3.26 us -> 0.01 us
    another operation x2 -> x0, local copies, waits for them, and re-layouts: 2.28 us -> none  [the longest x1 2.19 us: local(): query_flat = queries[:, 0].reshape(queries.shape[0], row_count * rank_full)]
  transfers between devices with their start and end apart: 3 -> 0, of which waited for: 3 -> 0; matrix products, arithmetic and copies ran while one was open for 8% -> 0% of each run, Pallas kernels for 0% -> 0%
where the time goes in v1:
time: 21.4 us; the launch traced here: 21.2 us
  Pallas kernels  19.3 us (90%)
  other arithmetic  1.25 us (6%)
  between operations  0.68 us (3%)
    pallas_call x1, Pallas kernels, local(): pl.pallas_call(functools.partial(kernel, (dp, pipe, tensor, x_chunks, g_c...  19.3 us
    transpose x1, other arithmetic, local(): return jnp.where(hits, 0.0, scores).T  1.25 us

profile of v1, /device:TPU:0, one launch (start us, length us, event | category | flops | bytes accessed | tf_op | source)
XLA Modules:
  0.0 21.2 jit_solution(10136293324642609524)
XLA Ops:
  0.7 0.0 copy-start
  0.7 19.3 %attribution.1 = f32[4,16]{1,0:T(4,128)} custom-call(bf16[1,512,2560]{2,1,0:T(8,128)(2,1)} %x_hbm.1, bf16[1,256,5120]{2,1,0:T(8,128)(2,1)} %g_hbm.1, bf16[1,64,2560]{2,1,0:T(8,128)(2,1)} %pin_hbm.1, bf16[1,64,5120]{2,1,0:T(8,128)(2,1)} %pout_hbm.1, s32[1]{0:T(128)S(6)} %copy.11.counts_hbm, s32[1,512]{1,0:T(1,128)} %bitcast.3, f32[1,64,64]{2,1,0:T(8,128)} %left_hbm.1, ...), custom_call_target="tpu_custom_call" | custom-call | tf_op jit(solution)/shard_map/attribution/pallas_call | solution.py:253
  20.0 0.0 copy-done
  20.0 1.3 %select_bitcast_fusion = f32[16,4]{0,1:T(4,128)} fusion(f32[4,16]{1,0:T(4,128)} %attribution.1, s32[16]{0:T(128)S(1)} %copy-done), kind=kLoop, calls=%fused_computation | loop fusion | flops 128 | bytes 576 | tf_op jit(solution)/shard_map/transpose | solution.py:289
Async XLA Ops:
  0.7 19.3 %copy-start = (s32[16]{0:T(128)S(1)}, s32[16]{0:T(128)}, u32[]{:S(2)}) copy-start(s32[16]{0:T(128)} %param.19) | copy-start | bytes 196

commit v2 on v1

--- a/solution.py
+++ b/solution.py
@@ -37,6 +37,8 @@
     left_v,
     right_v,
     q_v,
+    q_send,
+    q_recv,
     outs,
     p_send,
     p_recv,
@@ -49,6 +51,8 @@
     a_recv_sem,
     b_send_sem,
     b_recv_sem,
+    q_send_sem,
+    q_recv_sem,
     c_send_sem,
     c_recv_sem,
 ):
@@ -57,7 +61,8 @@
     rank = pout_v.shape[0]
     own_tok = g_v.shape[0]
     rows = rank // tensor
-    nq = q_v.shape[0]
+    nq = q_v.shape[0] // (pipe * tensor)
+    pairs = rows // 2
 
     def shift(i, by, size):
         return lax.rem(i + by, size)
@@ -77,6 +82,8 @@
     load_count.start()
     load_mask.start()
     load_pin.start()
+    load_q = pltpu.make_async_copy(q_hbm.at[:, 0], q_v, load_sem.at[6])
+    load_q.start()
     x_loads = []
     x_width = x_v.shape[1] // x_chunks
     for c in range(x_chunks):
@@ -86,26 +93,20 @@
         x_loads.append(load)
     load_left = pltpu.make_async_copy(left_hbm.at[0], left_v, load_sem.at[4])
     load_right = pltpu.make_async_copy(right_hbm.at[0], right_v, load_sem.at[5])
-    load_q = pltpu.make_async_copy(q_hbm.at[:, 0], q_v, load_sem.at[6])
     load_left.start()
     load_right.start()
-    load_q.start()
 
     barrier = pltpu.get_barrier_semaphore()
     block_peers = [(i, j) for i in range(dp) for j in range(tensor) if (i, j) != (0, 0)]
-    score_peers = [(i, j) for i in range(pipe) for j in range(tensor) if (i, j) != (0, 0)]
     met = 0
     for i, j in block_peers:
         pl.semaphore_signal(
             barrier, inc=1, device_id={"dp": shift(d, i, dp), "tensor": shift(t, j, tensor)}, device_id_type=MESH
         )
         met += 1
-    for i, j in score_peers:
-        if i:
-            pl.semaphore_signal(
-                barrier, inc=1, device_id={"pipe": shift(p, i, pipe), "tensor": shift(t, j, tensor)}, device_id_type=MESH
-            )
-            met += 1
+    for i in range(1, pipe):
+        pl.semaphore_signal(barrier, inc=1, device_id={"pipe": shift(p, i, pipe)}, device_id_type=MESH)
+        met += 1
 
     load_pout.wait()
     total = jnp.zeros((rank, own_tok), jnp.float32)
@@ -134,6 +135,29 @@
         copy.start()
         a_copies.append(copy)
 
+    load_q.wait()
+
+    def packed(owner):
+        parts = [q_v[pl.ds((i * tensor + owner) * nq, nq)] for i in range(pipe)]
+        both = jnp.concatenate(parts, axis=0)
+        both = jnp.concatenate([both[:, :pairs], both[:, pairs:]], axis=-1)
+        return both.reshape(q_send.shape[1:])
+
+    for j in range(1, tensor):
+        other = shift(t, j, tensor)
+        q_send[other] = packed(other)
+        copy = pltpu.make_async_remote_copy(
+            src_ref=q_send.at[other],
+            dst_ref=q_recv.at[t],
+            send_sem=q_send_sem.at[j],
+            recv_sem=q_recv_sem.at[t],
+            device_id={"tensor": other},
+            device_id_type=MESH,
+        )
+        copy.start()
+        a_copies.append(copy)
+    q_recv[t] = packed(t)
+
     load_pin.wait()
     ins = jnp.zeros((rank, x_v.shape[0]), jnp.float32)
     for c in range(x_chunks):
@@ -157,13 +181,14 @@
         grads += dot_nt(outs[j], ins[:, j * own_tok : (j + 1) * own_tok], HIGHEST)
     half = jnp.dot(left_v[...], grads, precision=HIGHEST, preferred_element_type=jnp.float32)
     block = jnp.dot(half, right_v[...], precision=HIGHEST, preferred_element_type=jnp.float32)
-    p_send[...] = block.reshape(tensor, rows, rank)
+    block = block.reshape(tensor, 2, pairs, rank)
+    p_send[...] = jnp.concatenate([block[:, 0], block[:, 1]], axis=-1)
 
     b_copies = []
     for i, j in block_peers:
         other = shift(t, j, tensor)
         copy = pltpu.make_async_remote_copy(
-            src_ref=p_send.at[other],
+            src_ref=p_send,
             dst_ref=p_recv.at[d, t],
             send_sem=b_send_sem.at[i, j],
             recv_sem=b_recv_sem.at[d, t],
@@ -172,12 +197,21 @@
         )
         copy.start()
         b_copies.append(copy)
-    p_recv[d, t] = p_send[t]
-    load_q.wait()
+    p_recv[d, t] = p_send[...]
+    for j in range(1, tensor):
+        source = shift(t, j, tensor)
+        pltpu.make_async_remote_copy(
+            src_ref=q_send.at[source],
+            dst_ref=q_recv.at[source],
+            send_sem=q_send_sem.at[j],
+            recv_sem=q_recv_sem.at[source],
+            device_id={"tensor": source},
+            device_id_type=MESH,
+        ).wait_recv()
     for i, j in block_peers:
         from_d, from_t = shift(d, i, dp), shift(t, j, tensor)
         pltpu.make_async_remote_copy(
-            src_ref=p_send.at[from_t],
+            src_ref=p_send,
             dst_ref=p_recv.at[from_d, from_t],
             send_sem=b_send_sem.at[i, j],
             recv_sem=b_recv_sem.at[from_d, from_t],
@@ -187,48 +221,48 @@
     precond = p_recv[:, 0]
     for j in range(1, tensor):
         precond += p_recv[:, j]
-    precond = precond.astype(jnp.bfloat16).reshape(dp * rows, rank)
-
-    lanes = dp * rows
-    products = dot_nt(q_v[...].reshape(nq * rows, rank), precond).reshape(nq, rows, lanes)
-    row = lax.broadcasted_iota(jnp.int32, (rows, lanes), 0)
-    lane = lax.broadcasted_iota(jnp.int32, (rows, lanes), 1)
-    same = (lax.rem(lane, rows) == row)[None]
+    lanes = dp * pairs
+    products = jnp.zeros((pipe * nq * pairs, lanes), jnp.float32)
+    for j in range(tensor):
+        share = precond[:, j].reshape(lanes, 2 * rank).astype(jnp.bfloat16)
+        products += dot_nt(q_recv[j], share)
+    products = products.reshape(pipe * nq, pairs, lanes)
+    row = lax.broadcasted_iota(jnp.int32, (pairs, lanes), 0)
+    lane = lax.broadcasted_iota(jnp.int32, (pairs, lanes), 1)
+    same = (lax.rem(lane, pairs) == row)[None]
     sums = jnp.sum(jnp.where(same, products, 0.0), axis=1)
     s_send[...] = sums.reshape(s_send.shape)
 
-    mine = p * tensor + t
     c_copies = []
-    for i, j in score_peers:
-        to_p, to_t = shift(p, i, pipe), shift(t, j, tensor)
+    for i in range(1, pipe):
+        other = shift(p, i, pipe)
         copy = pltpu.make_async_remote_copy(
-            src_ref=s_send.at[to_p * tensor + to_t],
-            dst_ref=s_recv.at[mine],
-            send_sem=c_send_sem.at[i, j],
-            recv_sem=c_recv_sem.at[mine],
-            device_id={"pipe": to_p, "tensor": to_t},
+            src_ref=s_send.at[other],
+            dst_ref=s_recv.at[p],
+            send_sem=c_send_sem.at[i],
+            recv_sem=c_recv_sem.at[p],
+            device_id={"pipe": other},
             device_id_type=MESH,
         )
         copy.start()
         c_copies.append(copy)
-    s_recv[mine] = s_send[mine]
-    for i, j in score_peers:
-        from_p, from_t = shift(p, i, pipe), shift(t, j, tensor)
-        source = from_p * tensor + from_t
+    s_recv[p] = s_send[p]
+    for i in range(1, pipe):
+        source = shift(p, i, pipe)
         pltpu.make_async_remote_copy(
             src_ref=s_send.at[source],
             dst_ref=s_recv.at[source],
-            send_sem=c_send_sem.at[i, j],
+            send_sem=c_send_sem.at[i],
             recv_sem=c_recv_sem.at[source],
-            device_id={"pipe": from_p, "tensor": from_t},
+            device_id={"pipe": source},
             device_id_type=MESH,
         ).wait_recv()
     scores = s_recv[0]
-    for i in range(1, pipe * tensor):
+    for i in range(1, pipe):
         scores += s_recv[i]
     owner = lax.broadcasted_iota(jnp.int32, (dp, lanes), 0)
     lane = lax.broadcasted_iota(jnp.int32, (dp, lanes), 1)
-    gather = jnp.where(lax.div(lane, rows) == owner, 1.0, 0.0).astype(jnp.float32)
+    gather = jnp.where(lax.div(lane, pairs) == owner, 1.0, 0.0).astype(jnp.float32)
     out_ref[...] = dot_nt(gather, scores, HIGHEST)
     for copy in a_copies + b_copies + c_copies:
         copy.wait_send()
@@ -245,7 +279,7 @@
     rows = rank // tensor
     nq = queries.shape[0]
     parts = pipe * tensor
-    lanes = dp * rows
+    lanes = dp * rows // 2
     x_chunks, g_chunks = cut(x.shape[2]), cut(g.shape[2])
     f32, bf16 = jnp.float32, jnp.bfloat16
     hbm = pl.BlockSpec(memory_space=pltpu.HBM)
@@ -265,11 +299,13 @@
             pltpu.VMEM((rank, rank), f32),
             pltpu.VMEM((rank, rank), f32),
             pltpu.VMEM((nq, rows, rank), bf16),
+            pltpu.VMEM((tensor, pipe * (nq // parts) * rows // 2, 2 * rank), bf16),
+            pltpu.VMEM((tensor, pipe * (nq // parts) * rows // 2, 2 * rank), bf16),
             pltpu.VMEM((tensor, rank, g.shape[1]), f32),
-            pltpu.VMEM((tensor, rows, rank), f32),
-            pltpu.VMEM((dp, tensor, rows, rank), f32),
-            pltpu.VMEM((parts, nq // parts, lanes), f32),
-            pltpu.VMEM((parts, nq // parts, lanes), f32),
+            pltpu.VMEM((tensor, rows // 2, 2 * rank), f32),
+            pltpu.VMEM((dp, tensor, tensor, rows // 2, 2 * rank), f32),
+            pltpu.VMEM((pipe, nq // parts, lanes), f32),
+            pltpu.VMEM((pipe, nq // parts, lanes), f32),
             dma((7,)),
             dma((x_chunks,)),
             dma((g_chunks,)),
@@ -277,8 +313,10 @@
             dma((tensor,)),
             dma((dp, tensor)),
             dma((dp, tensor)),
-            dma((pipe, tensor)),
-            dma((parts,)),
+            dma((tensor,)),
+            dma((tensor,)),
+            dma((pipe,)),
+            dma((pipe,)),
         ],
         compiler_params=pltpu.CompilerParams(
             collective_id=0, has_side_effects=True, vmem_limit_bytes=60 * 1024 * 1024

time: 21.4 us -> 19.6 us (0.916)
  Pallas kernels: 19.3 us -> 17.5 us
    pallas_call x1, Pallas kernels: 19.3 us -> 17.5 us  [local(): pl.pallas_call(functools.partial(kernel, (dp, pipe, tensor, x_chunks, g_c...]
where the time goes in v2:
time: 19.6 us; the launch traced here: 19.4 us
  Pallas kernels  17.5 us (89%)
  other arithmetic  1.25 us (6%)
  between operations  0.68 us (3%)
    pallas_call x1, Pallas kernels, local(): pl.pallas_call(functools.partial(kernel, (dp, pipe, tensor, x_chunks, g_c...  17.5 us
    transpose x1, other arithmetic, local(): return jnp.where(hits, 0.0, scores).T  1.25 us

profile of v2, /device:TPU:0, one launch (start us, length us, event | category | flops | bytes accessed | tf_op | source)
XLA Modules:
  0.0 19.4 jit_solution(7721532874559950404)
XLA Ops:
  0.7 0.0 copy-start
  0.7 17.5 %attribution.1 = f32[4,16]{1,0:T(4,128)} custom-call(bf16[1,512,2560]{2,1,0:T(8,128)(2,1)} %x_hbm.1, bf16[1,256,5120]{2,1,0:T(8,128)(2,1)} %g_hbm.1, bf16[1,64,2560]{2,1,0:T(8,128)(2,1)} %pin_hbm.1, bf16[1,64,5120]{2,1,0:T(8,128)(2,1)} %pout_hbm.1, s32[1]{0:T(128)S(6)} %copy.11.counts_hbm, s32[1,512]{1,0:T(1,128)} %bitcast.3, f32[1,64,64]{2,1,0:T(8,128)} %left_hbm.1, ...), custom_call_target="tpu_custom_call" | custom-call | tf_op jit(solution)/shard_map/attribution/pallas_call | solution.py:287
  18.2 0.0 copy-done
  18.2 1.3 %select_bitcast_fusion = f32[16,4]{0,1:T(4,128)} fusion(f32[4,16]{1,0:T(4,128)} %attribution.1, s32[16]{0:T(128)S(1)} %copy-done), kind=kLoop, calls=%fused_computation | loop fusion | flops 128 | bytes 576 | tf_op jit(solution)/shard_map/transpose | solution.py:327
Async XLA Ops:
  0.7 17.5 %copy-start = (s32[16]{0:T(128)S(1)}, s32[16]{0:T(128)}, u32[]{:S(2)}) copy-start(s32[16]{0:T(128)} %param.19) | copy-start | bytes 196

commit v3 on v2

--- a/solution.py
+++ b/solution.py
@@ -67,6 +67,18 @@
     def shift(i, by, size):
         return lax.rem(i + by, size)
 
+    barrier = pltpu.get_barrier_semaphore()
+    block_peers = [(i, j) for i in range(dp) for j in range(tensor) if (i, j) != (0, 0)]
+    met = 0
+    for i, j in block_peers:
+        pl.semaphore_signal(
+            barrier, inc=1, device_id={"dp": shift(d, i, dp), "tensor": shift(t, j, tensor)}, device_id_type=MESH
+        )
+        met += 1
+    for i in range(1, pipe):
+        pl.semaphore_signal(barrier, inc=1, device_id={"pipe": shift(p, i, pipe)}, device_id_type=MESH)
+        met += 1
+
     load_pout = pltpu.make_async_copy(pout_hbm.at[0], pout_v, load_sem.at[0])
     load_pout.start()
     g_loads = []
@@ -96,18 +108,6 @@
     load_left.start()
     load_right.start()
 
-    barrier = pltpu.get_barrier_semaphore()
-    block_peers = [(i, j) for i in range(dp) for j in range(tensor) if (i, j) != (0, 0)]
-    met = 0
-    for i, j in block_peers:
-        pl.semaphore_signal(
-            barrier, inc=1, device_id={"dp": shift(d, i, dp), "tensor": shift(t, j, tensor)}, device_id_type=MESH
-        )
-        met += 1
-    for i in range(1, pipe):
-        pl.semaphore_signal(barrier, inc=1, device_id={"pipe": shift(p, i, pipe)}, device_id_type=MESH)
-        met += 1
-
     load_pout.wait()
     total = jnp.zeros((rank, own_tok), jnp.float32)
     for c in range(g_chunks):
@@ -143,6 +143,7 @@
         both = jnp.concatenate([both[:, :pairs], both[:, pairs:]], axis=-1)
         return both.reshape(q_send.shape[1:])
 
+    q_copies = []
     for j in range(1, tensor):
         other = shift(t, j, tensor)
         q_send[other] = packed(other)
@@ -154,8 +155,7 @@
             device_id={"tensor": other},
             device_id_type=MESH,
         )
-        copy.start()
-        a_copies.append(copy)
+        q_copies.append(copy)
     q_recv[t] = packed(t)
 
     load_pin.wait()
@@ -197,6 +197,8 @@
         )
         copy.start()
         b_copies.append(copy)
+    for copy in q_copies:
+        copy.start()
     p_recv[d, t] = p_send[...]
     for j in range(1, tensor):
         source = shift(t, j, tensor)
@@ -264,7 +266,7 @@
     lane = lax.broadcasted_iota(jnp.int32, (dp, lanes), 1)
     gather = jnp.where(lax.div(lane, pairs) == owner, 1.0, 0.0).astype(jnp.float32)
     out_ref[...] = dot_nt(gather, scores, HIGHEST)
-    for copy in a_copies + b_copies + c_copies:
+    for copy in a_copies + b_copies + q_copies + c_copies:
         copy.wait_send()
 
 

time: 19.6 us -> 19.1 us (0.974)
  Pallas kernels: 17.5 us -> 16.9 us
    pallas_call x1, Pallas kernels: 17.5 us -> 16.9 us  [local(): pl.pallas_call(functools.partial(kernel, (dp, pipe, tensor, x_chunks, g_c...]
where the time goes in v3:
time: 19.1 us; the launch traced here: 18.9 us
  Pallas kernels  16.9 us (88%)
  other arithmetic  1.25 us (7%)
  between operations  0.68 us (4%)
    pallas_call x1, Pallas kernels, local(): pl.pallas_call(functools.partial(kernel, (dp, pipe, tensor, x_chunks, g_c...  16.9 us
    transpose x1, other arithmetic, local(): return jnp.where(hits, 0.0, scores).T  1.25 us

profile of v3, /device:TPU:0, one launch (start us, length us, event | category | flops | bytes accessed | tf_op | source)
XLA Modules:
  0.0 18.9 jit_solution(10633993911543579720)
XLA Ops:
  0.7 0.0 copy-start
  0.7 16.9 %attribution.1 = f32[4,16]{1,0:T(4,128)} custom-call(bf16[1,512,2560]{2,1,0:T(8,128)(2,1)} %x_hbm.1, bf16[1,256,5120]{2,1,0:T(8,128)(2,1)} %g_hbm.1, bf16[1,64,2560]{2,1,0:T(8,128)(2,1)} %pin_hbm.1, bf16[1,64,5120]{2,1,0:T(8,128)(2,1)} %pout_hbm.1, s32[1]{0:T(128)S(6)} %copy.11.counts_hbm, s32[1,512]{1,0:T(1,128)} %bitcast.3, f32[1,64,64]{2,1,0:T(8,128)} %left_hbm.1, ...), custom_call_target="tpu_custom_call" | custom-call | tf_op jit(solution)/shard_map/attribution/pallas_call | solution.py:289
  17.6 0.0 copy-done
  17.6 1.3 %select_bitcast_fusion = f32[16,4]{0,1:T(4,128)} fusion(f32[4,16]{1,0:T(4,128)} %attribution.1, s32[16]{0:T(128)S(1)} %copy-done), kind=kLoop, calls=%fused_computation | loop fusion | flops 128 | bytes 576 | tf_op jit(solution)/shard_map/transpose | solution.py:329
Async XLA Ops:
  0.7 17.0 %copy-start = (s32[16]{0:T(128)S(1)}, s32[16]{0:T(128)}, u32[]{:S(2)}) copy-start(s32[16]{0:T(128)} %param.19) | copy-start | bytes 196
